TPU v7x, 32 devices: a whole 2x2x4 slice. The times are simulated.
32 devices in a mesh: state: 4 (over x, core), snap: 8 (over z, y).
Axes of the slice: x: 2, y: 2, z: 4, core: 2. Of those that a mesh axis runs over, the one named last changes fastest.
Arguments:
- direct: float32 [2048, 1024], P('state', 'snap'), may hold values from -6 to 6
- adjoint: float32 [2048, 1024], P('state', 'snap'), may hold values from -6 to 6
- cell_weight: float32 [2048], P('state'), may hold values from 0.006629126 to 0.06629126
- right_vecs: float32 [1024, 256], P('snap'), may hold values from -0.1875 to 0.1875
- left_vecs: float32 [1024, 256], P('snap'), may hold values from -0.1875 to 0.1875
- inv_root: float32 [256], replicated, may hold values from 0.5 to 2
Outputs:
- gram: float32 [1024, 1024], P('state', 'snap')
- bal_modes: float32 [2048, 256], P(('state', 'snap'))
- adj_modes: float32 [2048, 256], P(('state', 'snap'))
All inputs are finite; a program needn't handle non-finite values.
Results may differ from a plain program's by a relative error of at most 0.00013.
Values sent between devices are 32-bit elements; how exact they have to be, the bound alone decides.
A program may use at most 64 MiB of HBM per device.

v0:
```python
import jax
import jax.numpy as jnp
from jax import lax
from jax.sharding import PartitionSpec as P


def local(direct, adjoint, cell_weight, right_vecs, left_vecs, inv_root):
    weighted = adjoint * cell_weight[:, None]
    snap_count = lax.axis_size("snap")
    product = lax.dot_general(
        lax.all_gather(weighted, "snap", axis=1, tiled=True),
        direct,
        (((0,), (0,)), ((), ())),
        precision=lax.Precision.HIGHEST,
        preferred_element_type=jnp.float32,
    )
    gram = lax.psum_scatter(product, "state", scatter_dimension=0, tiled=True)
    bal_terms = jnp.dot(
        direct,
        right_vecs * inv_root[None, :],
        precision=lax.Precision.HIGHEST,
        preferred_element_type=jnp.float32,
    )
    adj_terms = jnp.dot(
        adjoint,
        left_vecs * inv_root[None, :],
        precision=lax.Precision.HIGHEST,
        preferred_element_type=jnp.float32,
    )
    bal_whole, adj_whole = lax.psum((bal_terms, adj_terms), "snap")
    mode_rows = direct.shape[0] // snap_count
    first_row = lax.axis_index("snap") * mode_rows
    bal_modes = lax.dynamic_slice_in_dim(bal_whole, first_row, mode_rows, 0)
    adj_modes = lax.dynamic_slice_in_dim(adj_whole, first_row, mode_rows, 0)
    return (gram, bal_modes, adj_modes)


def solution(mesh):
    in_specs = (
        P("state", "snap"),
        P("state", "snap"),
        P("state"),
        P("snap", None),
        P("snap", None),
        P(),
    )
    out_specs = (P("state", "snap"), P(("state", "snap"), None), P(("state", "snap"), None))
    return jax.shard_map(local, mesh=mesh, in_specs=in_specs, out_specs=out_specs, check_vma=False)
```

profile of v0, /device:TPU:10, one launch (start us, length us, event | category | flops | bytes accessed | tf_op | source)
XLA Modules:
  0.0 172.5 jit_solution(12222261226357934841)
XLA Ops:
  7.2 0.0 copy-start
  7.2 0.0 all-gather.2.cloned.1.call-start
  7.2 1.8 %broadcast_multiply_fusion = f32[512,128]{1,0:T(8,128)} fusion(f32[512,128]{1,0:T(8,128)} %param.7, f32[512]{0:T(512)} %param.8), kind=kLoop, calls=%fused_computation.4 | loop fusion | flops 65536 | bytes 526336 | tf_op jit(solution)/shard_map/mul | solution.py:8
  9.0 0.0 all-gather.2.cloned.1.call-update
  9.1 0.0 all-reduce.3.cloned.1.call-start
  9.1 2.4 %convolution_bitcast_fusion = f32[512,256]{0,1:T(8,128)} fusion(f32[512,128]{1,0:T(8,128)} %param.7, f32[128,256]{1,0:T(8,128)} %param.10, f32[256]{0:T(256)} %param.11), kind=kOutput, calls=%fused_computation | convolution fusion | flops 201359360 | bytes 918528 | tf_op jit(solution)/shard_map/dot_general | solution.py:24
  11.6 0.0 copy-done
  11.6 2.3 %convolution_bitcast_fusion.1 = f32[512,256]{0,1:T(8,128)} fusion(f32[512,128]{1,0:T(8,128)S(1)} %copy-done, f32[128,256]{1,0:T(8,128)} %param.9, f32[256]{0:T(256)} %param.11), kind=kOutput, calls=%fused_computation.1 | convolution fusion | flops 201359360 | bytes 918528 | tf_op jit(solution)/shard_map/dot_general | solution.py:18
  13.9 0.0 all-reduce.3.cloned.1.call-update
  13.9 0.0 reduce-scatter.2.cloned.1.call-start
  14.0 46.5 %all-gather.2.cloned.1.call-done = f32[512,1024]{1,0:T(8,128)} async-done(((f32[512,128]{1,0:T(8,128)}), f32[512,1024]{1,0:T(8,128)}) %all-gather.2.cloned.1.call-update) | async-done | bytes 2097168 | tf_op jit(solution)/shard_map/all_gather | solution.py:11
  60.5 5.8 %fusion.4 = f32[1024,128]{1,0:T(8,128)} fusion(f32[512,1024]{1,0:T(8,128)} %all-gather.2.cloned.1.call-done, f32[512,128]{1,0:T(8,128)S(1)} %copy-done), kind=kOutput, calls=%fused_computation.9 | convolution fusion | flops 805306368 | bytes 2883584 | tf_op jit(solution)/shard_map/dot_general | solution.py:10
  66.3 0.0 reduce-scatter.2.cloned.1.call-update
  66.3 75.6 %all-reduce.3.cloned.1.call-done = (f32[512,256]{0,1:T(8,128)}, f32[512,256]{0,1:T(8,128)}) async-done(((f32[512,256]{0,1:T(8,128)}, f32[512,256]{0,1:T(8,128)}), (f32[512,256]{0,1:T(8,128)}, f32[512,256]{0,1:T(8,128)})) %all-reduce.3.cloned.1.call-update) | async-done | bytes 1048592 | tf_op jit(solution)/shard_map/psum | solution.py:30
  141.9 1.1 constant_dynamic-slice_fusion
  143.0 0.7 copy.9
  143.8 0.7 copy.10
  144.5 21.5 %reduce-scatter.2.cloned.1.call-done = f32[256,128]{1,0:T(8,128)} async-done(((f32[1024,128]{1,0:T(8,128)}), f32[256,128]{1,0:T(8,128)}) %reduce-scatter.2.cloned.1.call-update) | async-done | bytes 131088 | tf_op jit(solution)/shard_map/reduce_scatter | solution.py:17
Async XLA Ops:
  7.2 4.4 %copy-start = (f32[512,128]{1,0:T(8,128)S(1)}, f32[512,128]{1,0:T(8,128)}, u32[]{:S(2)}) copy-start(f32[512,128]{1,0:T(8,128)} %param.6) | copy-start | bytes 786436
  7.2 53.3 %all-gather.2.cloned.1.call-start = ((), (), s32[]{:S(2)}) async-start(), calls=%async_computation.1 | async-start | bytes 2359296 | tf_op jit(solution)/shard_map/all_gather | solution.py:11
  9.1 132.9 %all-reduce.3.cloned.1.call-start = ((), (), s32[]{:S(2)}) async-start(), calls=%async_computation.3 | async-start | bytes 2097152 | tf_op jit(solution)/shard_map/psum | solution.py:30
  13.9 152.1 %reduce-scatter.2.cloned.1.call-start = ((), (), s32[]{:S(2)}) async-start(), calls=%async_computation.2 | async-start | bytes 655360 | tf_op jit(solution)/shard_map/reduce_scatter | solution.py:17
Sparse Core Ops, SparseCore 0:
  10.1 50.3 all-gather.1
  64.0 77.8 all-reduce.2
  145.2 20.7 reduce-scatter.1
where the time goes:
time: 175 us; the launch traced here: 173 us
  waiting for transfers between devices  144 us (82%)
  between operations  13.8 us (8%)
  matrix products  10.6 us (6%)
  local copies, waits for them, and re-layouts  2.53 us (1%)
  other arithmetic  1.82 us (1%)
    psum x1, waiting for transfers between devices, local(): bal_whole, adj_whole = lax.psum((bal_terms, adj_terms), 'snap')  75.6 us
    all_gather x1, waiting for transfers between devices, local(): lax.all_gather(weighted, 'snap', axis=1, tiled=True)  46.5 us
    reduce_scatter x1, waiting for transfers between devices, local(): gram = lax.psum_scatter(product, 'state', scatter_dimension=0, tiled=True)  21.5 us
    dot_general x1, matrix products, local(): lax.dot_general(lax.all_gather(weighted, 'snap', axis=1, tiled=True), dir...  5.82 us
  transfers between devices with their start and end apart: 3, of which 3 were waited for; matrix products, arithmetic and copies ran while one was open for 8% of the time, Pallas kernels for 0%

commit v1 on v0

v1 whole, which is shorter than its diff:
```python
import functools
import math

import jax
import jax.numpy as jnp
from jax import lax
from jax.experimental import pallas as pl
from jax.experimental.pallas import tpu as pltpu
from jax.sharding import PartitionSpec as P

MESH = pl.DeviceIdType.MESH
F32 = jnp.float32
BF16 = jnp.bfloat16


def split(x):
    high = x.astype(BF16)
    return high, (x - high.astype(F32)).astype(BF16)


def product(a, b, side):
    def one(x, y):
        return lax.dot_general(x, y, (((side,), (0,)), ((), ())), preferred_element_type=F32)

    return one(a[0], b[0]) + (one(a[0], b[1]) + one(a[1], b[0]))


def kernel(far_count, near_count, chunks, a_ref, d_ref, w_ref, r_ref, l_ref, root_ref,
           gram_ref, bal_ref, adj_ref,
           a_held, d_held, r_held, wd_high, wd_low, g_out, g_in, part, part_out, part_in, m_out, m_in,
           a_send, a_recv, d_send, d_recv, r_send, r_recv, g_send, g_recv, p_send, p_recv, m_send, m_recv):
    state = lax.axis_index("state")
    snap = lax.axis_index("snap")
    far, near = snap // near_count, snap % near_count
    rows, width = a_ref.shape[2], a_ref.shape[3]
    cells = far_count * near_count * rows
    modes = r_ref.shape[1]
    slab = far_count // chunks

    def near_of(k):
        return lax.rem(near + k, near_count)

    def snap_of(far_at, near_at):
        return far_at * near_count + near_at

    barrier = pltpu.get_barrier_semaphore()

    def greet(k, carry):
        other = lax.rem(state + k // near_count, far_count)
        beside = lax.rem(near + k % near_count, near_count)
        pl.semaphore_signal(barrier, inc=1, device_id=(other, snap_of(far, beside)), device_id_type=MESH)
        return carry

    lax.fori_loop(1, far_count * near_count, greet, 0)

    def greet_far(k, carry):
        pl.semaphore_signal(barrier, inc=1, device_id=(state, snap_of(lax.rem(far + k, far_count), near)), device_id_type=MESH)
        return carry

    lax.fori_loop(1, far_count, greet_far, 0)
    pl.semaphore_wait(barrier, far_count * near_count - 1 + far_count - 1)

    def a_copy(way, step, chunk, src, block):
        go = 1 if way == 0 else -1
        at = pl.ds(chunk * slab, slab)
        return pltpu.make_async_remote_copy(
            src_ref=src.at[at],
            dst_ref=a_held.at[block, at],
            send_sem=a_send.at[way, step, chunk],
            recv_sem=a_recv.at[way, step, chunk],
            device_id=(state, snap_of(jnp.clip(far + go, 0, far_count - 1), near)),
            device_id_type=MESH,
        )

    has_next = (far < far_count - 1, far > 0)

    for chunk in range(chunks):
        for way in range(2):
            @pl.when(has_next[way])
            def _():
                a_copy(way, 0, chunk, a_ref, far).start()

    def d_copy(k):
        return pltpu.make_async_remote_copy(
            src_ref=d_ref, dst_ref=d_held.at[near], send_sem=d_send.at[k], recv_sem=d_recv.at[k],
            device_id=(state, snap_of(far, near_of(k))), device_id_type=MESH)

    def r_copy(k):
        return pltpu.make_async_remote_copy(
            src_ref=r_ref, dst_ref=r_held.at[near], send_sem=r_send.at[k], recv_sem=r_recv.at[k],
            device_id=(state, snap_of(far, near_of(k))), device_id_type=MESH)

    def p_copy(k):
        return pltpu.make_async_remote_copy(
            src_ref=part_out.at[k], dst_ref=part_in.at[k], send_sem=p_send.at[k], recv_sem=p_recv.at[k],
            device_id=(state, snap_of(far, near_of(k))), device_id_type=MESH)

    for k in range(1, near_count):
        d_copy(k).start()
        r_copy(k).start()

    root = root_ref[...]
    left = split(l_ref[...] * root)

    def adjoint_terms(near_at):
        x = a_ref[:, near_at].reshape(far_count * rows, width)
        return product(split(x), left, 1).reshape(far_count, rows, modes)

    for k in range(1, near_count):
        part_out[k] = adjoint_terms(near_of(k))
        p_copy(k).start()
    part[...] = adjoint_terms(near)

    def pass_on(step):
        for chunk in range(chunks):
            for way in range(2):
                block = far - step if way == 0 else far + step
                held = jnp.clip(block, 0, far_count - 1)

                @pl.when((block >= 0) & (block < far_count))
                def _():
                    a_copy(way, step - 1, chunk, a_ref, held).wait_recv()

                    @pl.when(has_next[way])
                    def _():
                        a_copy(way, step, chunk, a_held.at[held], held).start()

    def g_copy(block, beside):
        return pltpu.make_async_remote_copy(
            src_ref=g_out.at[block, beside], dst_ref=g_in.at[state, near],
            send_sem=g_send.at[block, beside], recv_sem=g_recv.at[state, near],
            device_id=(block, snap_of(far, beside)), device_id_type=MESH)

    def gram_block(value, block):
        x = split(value.reshape(cells, width))
        whole = product(x, (wd_high[...], wd_low[...]), 0)
        for beside in range(near_count):
            piece = whole[:, beside * width:(beside + 1) * width]
            own = (block == state) & (beside == near)

            @pl.when(own)
            def _():
                g_in[state, near] = piece

            @pl.when(jnp.logical_not(own))
            def _():
                g_out[block, beside] = piece
                g_copy(block, beside).start()

    def gram_step(step):
        for way in range(2):
            block = far - step if way == 0 else far + step
            held = jnp.clip(block, 0, far_count - 1)

            @pl.when((block >= 0) & (block < far_count))
            def _():
                gram_block(a_held[held], held)

    pass_on(1)

    for k in range(1, near_count):
        d_copy(k).wait_recv()
    d_held[near] = d_ref[...]
    weight = jnp.broadcast_to(w_ref[...], (width, cells)).T
    for beside in range(near_count):
        high, low = split(d_held[beside].reshape(cells, width) * weight)
        wd_high[:, beside * width:(beside + 1) * width] = high
        wd_low[:, beside * width:(beside + 1) * width] = low
    gram_block(a_ref[...], far)
    gram_step(1)
    if far_count > 2:
        pass_on(2)

    for k in range(1, near_count):
        r_copy(k).wait_recv()
    r_held[near] = r_ref[...]
    total = None
    for beside in range(near_count):
        x = d_held[beside, :, near].reshape(far_count * rows, width)
        term = product(split(x), split(r_held[beside] * root), 1)
        total = term if total is None else total + term
    m_out[:, 0] = total.reshape(far_count, rows, modes)
    total = part[...]
    for k in range(1, near_count):
        p_copy(k).wait_recv()
        total = total + part_in[k]
    m_out[:, 1] = total

    def m_copy(k):
        other = lax.rem(far + k, far_count)
        return pltpu.make_async_remote_copy(
            src_ref=m_out.at[other], dst_ref=m_in.at[k], send_sem=m_send.at[k], recv_sem=m_recv.at[k],
            device_id=(state, snap_of(other, near)), device_id_type=MESH)

    def each_far(first, body):
        def step(k, carry):
            body(k)
            return carry

        lax.fori_loop(first, far_count, step, 0)

    each_far(1, lambda k: m_copy(k).start())

    if far_count > 2:
        gram_step(2)

    def later(step):
        pass_on(step)
        gram_step(step)

    each_far(3, later)

    m_in[0] = m_out[far]
    each_far(1, lambda k: m_copy(k).wait_recv())
    bal_ref[...] = jnp.sum(m_in[:, 0], axis=0)
    adj_ref[...] = jnp.sum(m_in[:, 1], axis=0)

    def g_wait(k):
        source, beside = k // near_count, k % near_count

        @pl.when((source != state) | (beside != near))
        def _():
            pltpu.make_async_remote_copy(
                src_ref=g_out.at[source, beside], dst_ref=g_in.at[source, beside],
                send_sem=g_send.at[source, beside], recv_sem=g_recv.at[source, beside],
                device_id=(source, snap_of(far, beside)), device_id_type=MESH).wait_recv()

    lax.fori_loop(0, far_count * near_count, lambda k, c: (g_wait(k), c)[1], 0)
    for beside in range(near_count):
        gram_ref[beside] = jnp.sum(g_in[:, beside], axis=0)

    for k in range(1, near_count):
        d_copy(k).wait_send()
        r_copy(k).wait_send()
        p_copy(k).wait_send()
    each_far(1, lambda k: m_copy(k).wait_send())

    def g_left(k):
        block, beside = k // near_count, k % near_count

        @pl.when((block != state) | (beside != near))
        def _():
            g_copy(block, beside).wait_send()

    lax.fori_loop(0, far_count * near_count, lambda k, c: (g_left(k), c)[1], 0)

    def a_left(step):
        for chunk in range(chunks):
            for way in range(2):
                block = far - step if way == 0 else far + step

                @pl.when((block >= 0) & (block < far_count) & has_next[way])
                def _():
                    a_copy(way, step, chunk, a_ref, far).wait_send()

    each_far(0, a_left)


def local(direct, adjoint, cell_weight, right_vecs, left_vecs, inv_root):
    far_count = lax.axis_size("state")
    near_count = lax.axis_size("snap") // far_count
    cells, width = direct.shape
    modes = right_vecs.shape[1]
    rows = cells // (far_count * near_count)
    chunks = math.gcd(far_count, 4)
    block = (far_count, near_count, rows, width)
    vmem = pl.BlockSpec(memory_space=pltpu.VMEM)
    dma = pltpu.SemaphoreType.DMA
    gram, bal, adj = pl.pallas_call(
        functools.partial(kernel, far_count, near_count, chunks),
        out_shape=(
            jax.ShapeDtypeStruct((near_count, width, width), F32),
            jax.ShapeDtypeStruct((rows, modes), F32),
            jax.ShapeDtypeStruct((rows, modes), F32),
        ),
        in_specs=[vmem] * 6,
        out_specs=(vmem,) * 3,
        scratch_shapes=[
            pltpu.VMEM((far_count,) + block, F32),
            pltpu.VMEM((near_count,) + block, F32),
            pltpu.VMEM((near_count, width, modes), F32),
            pltpu.VMEM((cells, near_count * width), BF16),
            pltpu.VMEM((cells, near_count * width), BF16),
            pltpu.VMEM((far_count, near_count, width, width), F32),
            pltpu.VMEM((far_count, near_count, width, width), F32),
            pltpu.VMEM((far_count, rows, modes), F32),
            pltpu.VMEM((near_count, far_count, rows, modes), F32),
            pltpu.VMEM((near_count, far_count, rows, modes), F32),
            pltpu.VMEM((far_count, 2, rows, modes), F32),
            pltpu.VMEM((far_count, 2, rows, modes), F32),
            dma((2, far_count, chunks)),
            dma((2, far_count, chunks)),
            dma((near_count,)),
            dma((near_count,)),
            dma((near_count,)),
            dma((near_count,)),
            dma((far_count, near_count)),
            dma((far_count, near_count)),
            dma((near_count,)),
            dma((near_count,)),
            dma((far_count,)),
            dma((far_count,)),
        ],
        compiler_params=pltpu.CompilerParams(
            collective_id=0, has_side_effects=True, vmem_limit_bytes=48 * 1024 * 1024
        ),
    )(
        adjoint.reshape(block),
        direct.reshape(block),
        cell_weight.reshape(1, cells),
        right_vecs,
        left_vecs,
        inv_root.reshape(1, modes),
    )
    return gram.reshape(near_count * width, width), bal, adj


def solution(mesh):
    in_specs = (
        P("state", "snap"),
        P("state", "snap"),
        P("state"),
        P("snap", None),
        P("snap", None),
        P(),
    )
    out_specs = (P("state", "snap"), P(("state", "snap"), None), P(("state", "snap"), None))
    return jax.shard_map(local, mesh=mesh, in_specs=in_specs, out_specs=out_specs, check_vma=False)
```

time: 175 us -> 41.7 us (0.24); the launches traced: 173 us -> 41.3 us
  waiting for transfers between devices: 144 us -> 0 us
  Pallas kernels: 0 us -> 34.3 us
  between operations: 13.8 us -> 0.66 us
  matrix products: 10.6 us -> 0 us
  local copies, waits for them, and re-layouts: 2.53 us -> 6.3 us
  other arithmetic: 1.82 us -> 0 us
    psum x1 -> x0, waiting for transfers between devices: 75.6 us -> none  [local(): bal_whole, adj_whole = lax.psum((bal_terms, adj_terms), 'snap')]
    all_gather x1 -> x0, waiting for transfers between devices: 46.5 us -> none  [local(): lax.all_gather(weighted, 'snap', axis=1, tiled=True)]
    pallas_call x0 -> x1, Pallas kernels: none -> 34.3 us  [local(): pl.pallas_call(functools.partial(kernel, far_count, near_count, chunks),...]
    reduce_scatter x1 -> x0, waiting for transfers between devices: 21.5 us -> none  [local(): gram = lax.psum_scatter(product, 'state', scatter_dimension=0, tiled=True)]
    dot_general x3 -> x0, matrix products: 10.6 us -> none  [the longest x1 5.82 us: local(): lax.dot_general(lax.all_gather(weighted, 'snap', axis=1, tiled=True), dir...]
    unnamed x4 -> x15, local copies, waits for them, and re-layouts: 1.44 us -> 6.3 us
    mul x1 -> x0, other arithmetic: 1.82 us -> none  [local(): weighted = adjoint * cell_weight[:, None]]
  transfers between devices with their start and end apart: 3 -> 0, of which waited for: 3 -> 0; matrix products, arithmetic and copies ran while one was open for 8% -> 0% of each run, Pallas kernels for 0% -> 0%
where the time goes in v1:
time: 41.7 us; the launch traced here: 41.3 us
  Pallas kernels  34.3 us (82%)
  local copies, waits for them, and re-layouts  6.3 us (15%)
  between operations  0.66 us (2%)
    pallas_call x1, Pallas kernels, local(): pl.pallas_call(functools.partial(kernel, far_count, near_count, chunks),...  34.3 us
    unnamed x15, local copies, waits for them, and re-layouts  6.3 us

profile of v1, /device:TPU:10, one launch (start us, length us, event | category | flops | bytes accessed | tf_op | source)
XLA Modules:
  0.0 41.3 jit_solution(7487428772132536087)
XLA Ops:
  0.6 0.0 copy-start.4
  0.6 0.0 copy-start.5
  0.7 0.7 %copy-done.4 = f32[512]{0:T(512)S(1)} copy-done((f32[512]{0:T(512)S(1)}, f32[512]{0:T(512)}, u32[]{:S(2)}) %copy-start.4) | copy-done | bytes 2072
  1.3 0.0 copy-done.5
  1.3 0.0 copy-start
  1.3 0.9 %copy-done = f32[512,128]{1,0:T(8,128)S(1)} copy-done((f32[512,128]{1,0:T(8,128)S(1)}, f32[512,128]{1,0:T(8,128)}, u32[]{:S(2)}) %copy-start) | copy-done | bytes 262168
  2.3 0.0 copy-start.1
  2.3 0.9 %copy-done.1 = f32[512,128]{1,0:T(8,128)S(1)} copy-done((f32[512,128]{1,0:T(8,128)S(1)}, f32[512,128]{1,0:T(8,128)}, u32[]{:S(2)}) %copy-start.1) | copy-done | bytes 262168
  3.2 0.0 copy-start.2
  3.2 0.9 %copy-done.2 = f32[128,256]{1,0:T(8,128)S(1)} copy-done((f32[128,256]{1,0:T(8,128)S(1)}, f32[128,256]{1,0:T(8,128)}, u32[]{:S(2)}) %copy-start.2) | copy-done | bytes 131096
  4.1 0.0 copy-start.3
  4.1 0.9 %copy-done.3 = f32[128,256]{1,0:T(8,128)S(1)} copy-done((f32[128,256]{1,0:T(8,128)S(1)}, f32[128,256]{1,0:T(8,128)}, u32[]{:S(2)}) %copy-start.3) | copy-done | bytes 131096
  5.0 34.3 %shard_map.85 = (f32[2,128,128]{2,1,0:T(8,128)S(1)}, f32[64,256]{1,0:T(8,128)S(1)}, f32[64,256]{1,0:T(8,128)S(1)}) custom-call(f32[4,2,64,128]{3,2,1,0:T(8,128)S(1)} %bitcast.5, f32[4,2,64,128]{3,2,1,0:T(8,128)S(1)} %bitcast.6, f32[1,512]{1,0:T(1,128)S(1)} %bitcast.8, f32[128,256]{1,0:T(8,128)S(1)} %copy-done.2, f32[128,256]{1,0:T(8,128)S(1)} %copy-done.3, ...), custom_call_target="tpu_custom_call" | custom-call | tf_op jit(solution)/shard_map/pallas_call | solution.py:269
  39.4 0.7 %copy.12 = f32[256,128]{1,0:T(8,128)} copy(f32[256,128]{1,0:T(8,128)S(1)} %bitcast.7) | data formatting | bytes 262144
  40.0 0.6 %copy.13 = f32[64,256]{1,0:T(8,128)} copy(f32[64,256]{1,0:T(8,128)S(1)} %get-tuple-element.13) | data formatting | bytes 131072
  40.7 0.6 %copy.14 = f32[64,256]{1,0:T(8,128)} copy(f32[64,256]{1,0:T(8,128)S(1)} %get-tuple-element.14) | data formatting | bytes 131072
Async XLA Ops:
  0.6 0.7 %copy-start.4 = (f32[512]{0:T(512)S(1)}, f32[512]{0:T(512)}, u32[]{:S(2)}) copy-start(f32[512]{0:T(512)} %param.8) | copy-start | bytes 6148
  0.6 0.7 %copy-start.5 = (f32[256]{0:T(256)S(1)}, f32[256]{0:T(256)}, u32[]{:S(2)}) copy-start(f32[256]{0:T(256)} %param.11) | copy-start | bytes 3076
  1.3 0.9 %copy-start = (f32[512,128]{1,0:T(8,128)S(1)}, f32[512,128]{1,0:T(8,128)}, u32[]{:S(2)}) copy-start(f32[512,128]{1,0:T(8,128)} %param.7) | copy-start | bytes 786436
  2.3 0.9 %copy-start.1 = (f32[512,128]{1,0:T(8,128)S(1)}, f32[512,128]{1,0:T(8,128)}, u32[]{:S(2)}) copy-start(f32[512,128]{1,0:T(8,128)} %param.6) | copy-start | bytes 786436
  3.2 0.9 %copy-start.2 = (f32[128,256]{1,0:T(8,128)S(1)}, f32[128,256]{1,0:T(8,128)}, u32[]{:S(2)}) copy-start(f32[128,256]{1,0:T(8,128)} %r_ref.1) | copy-start | bytes 393220
  4.1 0.9 %copy-start.3 = (f32[128,256]{1,0:T(8,128)S(1)}, f32[128,256]{1,0:T(8,128)}, u32[]{:S(2)}) copy-start(f32[128,256]{1,0:T(8,128)} %l_ref.1) | copy-start | bytes 393220

commit v2 on v1

--- a/solution.py
+++ b/solution.py
@@ -25,16 +25,16 @@
     return one(a[0], b[0]) + (one(a[0], b[1]) + one(a[1], b[0]))
 
 
-def kernel(far_count, near_count, chunks, a_ref, d_ref, w_ref, r_ref, l_ref, root_ref,
-           gram_ref, bal_ref, adj_ref,
+def kernel(far_count, near_count, chunks, a_hbm, d_hbm, w_hbm, r_hbm, l_hbm, root_hbm,
+           gram_ref, bal_ref, adj_ref, a_ref, l_ref, w_ref, root_ref, load_sem,
            a_held, d_held, r_held, wd_high, wd_low, g_out, g_in, part, part_out, part_in, m_out, m_in,
            a_send, a_recv, d_send, d_recv, r_send, r_recv, g_send, g_recv, p_send, p_recv, m_send, m_recv):
     state = lax.axis_index("state")
     snap = lax.axis_index("snap")
     far, near = snap // near_count, snap % near_count
-    rows, width = a_ref.shape[2], a_ref.shape[3]
+    rows, width = a_hbm.shape[2], a_hbm.shape[3]
     cells = far_count * near_count * rows
-    modes = r_ref.shape[1]
+    modes = r_hbm.shape[1]
     slab = far_count // chunks
 
     def near_of(k):
@@ -58,6 +58,15 @@
         return carry
 
     lax.fori_loop(1, far_count, greet_far, 0)
+    loads = [
+        pltpu.make_async_copy(src, dst, load_sem.at[i])
+        for i, (src, dst) in enumerate((
+            (l_hbm, l_ref), (root_hbm, root_ref), (a_hbm, a_ref), (w_hbm, w_ref),
+            (d_hbm, d_held.at[near]), (r_hbm, r_held.at[near]),
+        ))
+    ]
+    for load in loads:
+        load.start()
     pl.semaphore_wait(barrier, far_count * near_count - 1 + far_count - 1)
 
     def a_copy(way, step, chunk, src, block):
@@ -78,16 +87,16 @@
         for way in range(2):
             @pl.when(has_next[way])
             def _():
-                a_copy(way, 0, chunk, a_ref, far).start()
+                a_copy(way, 0, chunk, a_hbm, far).start()
 
     def d_copy(k):
         return pltpu.make_async_remote_copy(
-            src_ref=d_ref, dst_ref=d_held.at[near], send_sem=d_send.at[k], recv_sem=d_recv.at[k],
+            src_ref=d_hbm, dst_ref=d_held.at[near], send_sem=d_send.at[k], recv_sem=d_recv.at[k],
             device_id=(state, snap_of(far, near_of(k))), device_id_type=MESH)
 
     def r_copy(k):
         return pltpu.make_async_remote_copy(
-            src_ref=r_ref, dst_ref=r_held.at[near], send_sem=r_send.at[k], recv_sem=r_recv.at[k],
+            src_ref=r_hbm, dst_ref=r_held.at[near], send_sem=r_send.at[k], recv_sem=r_recv.at[k],
             device_id=(state, snap_of(far, near_of(k))), device_id_type=MESH)
 
     def p_copy(k):
@@ -99,6 +108,8 @@
         d_copy(k).start()
         r_copy(k).start()
 
+    for load in loads:
+        load.wait()
     root = root_ref[...]
     left = split(l_ref[...] * root)
 
@@ -160,7 +171,6 @@
 
     for k in range(1, near_count):
         d_copy(k).wait_recv()
-    d_held[near] = d_ref[...]
     weight = jnp.broadcast_to(w_ref[...], (width, cells)).T
     for beside in range(near_count):
         high, low = split(d_held[beside].reshape(cells, width) * weight)
@@ -173,7 +183,6 @@
 
     for k in range(1, near_count):
         r_copy(k).wait_recv()
-    r_held[near] = r_ref[...]
     total = None
     for beside in range(near_count):
         x = d_held[beside, :, near].reshape(far_count * rows, width)
@@ -254,6 +263,15 @@
                     a_copy(way, step, chunk, a_ref, far).wait_send()
 
     each_far(0, a_left)
+
+
+def deliver(gram_ref, bal_ref, adj_ref, gram_out, bal_out, adj_out, sem):
+    pairs = ((gram_ref, gram_out), (bal_ref, bal_out), (adj_ref, adj_out))
+    copies = [pltpu.make_async_copy(src, dst, sem.at[i]) for i, (src, dst) in enumerate(pairs)]
+    for copy in copies:
+        copy.start()
+    for copy in copies:
+        copy.wait()
 
 
 def local(direct, adjoint, cell_weight, right_vecs, left_vecs, inv_root):
@@ -266,16 +284,22 @@
     block = (far_count, near_count, rows, width)
     vmem = pl.BlockSpec(memory_space=pltpu.VMEM)
     dma = pltpu.SemaphoreType.DMA
-    gram, bal, adj = pl.pallas_call(
+    hbm = pl.BlockSpec(memory_space=pltpu.HBM)
+    results = pl.pallas_call(
         functools.partial(kernel, far_count, near_count, chunks),
         out_shape=(
             jax.ShapeDtypeStruct((near_count, width, width), F32),
             jax.ShapeDtypeStruct((rows, modes), F32),
             jax.ShapeDtypeStruct((rows, modes), F32),
         ),
-        in_specs=[vmem] * 6,
+        in_specs=[hbm] * 6,
         out_specs=(vmem,) * 3,
         scratch_shapes=[
+            pltpu.VMEM(block, F32),
+            pltpu.VMEM((width, modes), F32),
+            pltpu.VMEM((1, cells), F32),
+            pltpu.VMEM((1, modes), F32),
+            dma((6,)),
             pltpu.VMEM((far_count,) + block, F32),
             pltpu.VMEM((near_count,) + block, F32),
             pltpu.VMEM((near_count, width, modes), F32),
@@ -302,7 +326,7 @@
             dma((far_count,)),
         ],
         compiler_params=pltpu.CompilerParams(
-            collective_id=0, has_side_effects=True, vmem_limit_bytes=48 * 1024 * 1024
+            collective_id=0, has_side_effects=True, vmem_limit_bytes=63 * 1024 * 1024
         ),
     )(
         adjoint.reshape(block),
@@ -312,6 +336,14 @@
         left_vecs,
         inv_root.reshape(1, modes),
     )
+    gram, bal, adj = pl.pallas_call(
+        deliver,
+        out_shape=tuple(jax.ShapeDtypeStruct(r.shape, F32) for r in results),
+        in_specs=[hbm] * 3,
+        out_specs=(hbm,) * 3,
+        scratch_shapes=[dma((3,))],
+        compiler_params=pltpu.CompilerParams(vmem_limit_bytes=63 * 1024 * 1024),
+    )(*results)
     return gram.reshape(near_count * width, width), bal, adj
 
 

time: 41.7 us -> 45.4 us (1.089)
  Pallas kernels: 34.3 us -> 44.6 us
  local copies, waits for them, and re-layouts: 6.3 us -> 0 us
    pallas_call x0 -> x1, Pallas kernels: none -> 9.07 us  [local(): pl.pallas_call(deliver, out_shape=tuple((jax.ShapeDtypeStruct(r.shape, F3...]
    unnamed x15 -> x0, local copies, waits for them, and re-layouts: 6.3 us -> none
    pallas_call x1, Pallas kernels: 34.3 us -> 35.5 us  [local(): pl.pallas_call(functools.partial(kernel, far_count, near_count, chunks),...]
where the time goes in v2:
time: 45.4 us; the launch traced here: 45.2 us
  Pallas kernels  44.6 us (98%)
  between operations  0.64 us (1%)
    pallas_call x1, Pallas kernels, local(): pl.pallas_call(functools.partial(kernel, far_count, near_count, chunks),...  35.5 us
    pallas_call x1, Pallas kernels, local(): pl.pallas_call(deliver, out_shape=tuple((jax.ShapeDtypeStruct(r.shape, F3...  9.07 us

profile of v2, /device:TPU:10, one launch (start us, length us, event | category | flops | bytes accessed | tf_op | source)
XLA Modules:
  0.0 45.2 jit_solution(6751697964942465971)
XLA Ops:
  0.6 35.5 %shard_map.85 = (f32[2,128,128]{2,1,0:T(8,128)}, f32[64,256]{1,0:T(8,128)}, f32[64,256]{1,0:T(8,128)}) custom-call(f32[4,2,64,128]{3,2,1,0:T(8,128)} %bitcast.5, f32[4,2,64,128]{3,2,1,0:T(8,128)} %bitcast.6, f32[1,512]{1,0:T(1,128)} %bitcast.7, f32[128,256]{1,0:T(8,128)} %r_hbm.1, f32[128,256]{1,0:T(8,128)} %l_hbm.1, f32[1,256]{1,0:T(1,128)} %bitcast.8), custom_call_target="tpu_custom_call" | custom-call | tf_op jit(solution)/shard_map/pallas_call | solution.py:288
  36.2 9.1 %shard_map.86 = (f32[2,128,128]{2,1,0:T(8,128)}, f32[64,256]{1,0:T(8,128)}, f32[64,256]{1,0:T(8,128)}) custom-call(f32[2,128,128]{2,1,0:T(8,128)} %get-tuple-element.9.gram_ref, f32[64,256]{1,0:T(8,128)} %get-tuple-element.10.bal_ref, f32[64,256]{1,0:T(8,128)} %get-tuple-element.11.adj_ref), custom_call_target="tpu_custom_call" | custom-call | tf_op jit(solution)/shard_map/pallas_call | solution.py:339

commit v3 on v2

--- a/solution.py
+++ b/solution.py
@@ -27,7 +27,7 @@
 
 def kernel(far_count, near_count, chunks, a_hbm, d_hbm, w_hbm, r_hbm, l_hbm, root_hbm,
            gram_ref, bal_ref, adj_ref, a_ref, l_ref, w_ref, root_ref, load_sem,
-           a_held, d_held, r_held, wd_high, wd_low, g_out, g_in, part, part_out, part_in, m_out, m_in,
+           a_held, d_held, r_held, wd_high, wd_low, g_out, g_in, part, part_out, part_in, m_out, m_in, sums,
            a_send, a_recv, d_send, d_recv, r_send, r_recv, g_send, g_recv, p_send, p_recv, m_send, m_recv):
     state = lax.axis_index("state")
     snap = lax.axis_index("snap")
@@ -144,7 +144,9 @@
 
     def gram_block(value, block):
         x = split(value.reshape(cells, width))
-        whole = product(x, (wd_high[...], wd_low[...]), 0)
+        hand_out(product(x, (wd_high[...], wd_low[...]), 0), block)
+
+    def hand_out(whole, block):
         for beside in range(near_count):
             piece = whole[:, beside * width:(beside + 1) * width]
             own = (block == state) & (beside == near)
@@ -157,6 +159,31 @@
             def _():
                 g_out[block, beside] = piece
                 g_copy(block, beside).start()
+
+    def pass_and_add(step):
+        for chunk in range(chunks):
+            for way in range(2):
+                block = far - step if way == 0 else far + step
+                held = jnp.clip(block, 0, far_count - 1)
+
+                @pl.when((block >= 0) & (block < far_count))
+                def _():
+                    a_copy(way, step - 1, chunk, a_ref, held).wait_recv()
+
+                    @pl.when(has_next[way])
+                    def _():
+                        a_copy(way, step, chunk, a_held.at[held], held).start()
+
+                    size = cells // chunks
+                    x = split(a_held[held, pl.ds(chunk * slab, slab)].reshape(size, width))
+                    at = pl.ds(chunk * size, size)
+                    terms = product(x, (wd_high[at], wd_low[at]), 0)
+                    if chunk > 0:
+                        terms = terms + sums[way]
+                    if chunk < chunks - 1:
+                        sums[way] = terms
+                    else:
+                        hand_out(terms, held)
 
     def gram_step(step):
         for way in range(2):
@@ -179,7 +206,7 @@
     gram_block(a_ref[...], far)
     gram_step(1)
     if far_count > 2:
-        pass_on(2)
+        pass_and_add(2)
 
     for k in range(1, near_count):
         r_copy(k).wait_recv()
@@ -195,11 +222,13 @@
         total = total + part_in[k]
     m_out[:, 1] = total
 
-    def m_copy(k):
-        other = lax.rem(far + k, far_count)
-        return pltpu.make_async_remote_copy(
-            src_ref=m_out.at[other], dst_ref=m_in.at[k], send_sem=m_send.at[k], recv_sem=m_recv.at[k],
-            device_id=(state, snap_of(other, near)), device_id_type=MESH)
+    def m_copy(way, at, src):
+        go = 1 if way == 0 else -1
+        return pltpu.make_async_remote_copy(
+            src_ref=src, dst_ref=m_in.at[way, at], send_sem=m_send.at[way, at], recv_sem=m_recv.at[way, at],
+            device_id=(state, snap_of(jnp.clip(far + go, 0, far_count - 1), near)), device_id_type=MESH)
+
+    has_before = (has_next[1], has_next[0])
 
     def each_far(first, body):
         def step(k, carry):
@@ -208,21 +237,52 @@
 
         lax.fori_loop(first, far_count, step, 0)
 
-    each_far(1, lambda k: m_copy(k).start())
-
+    def stage(k):
+        for way in range(2):
+            @pl.when(far == (k if way == 0 else far_count - 1 - k))
+            def _():
+                def one(j):
+                    at = far_count - j if way == 0 else j - 1
+                    beyond = at > far if way == 0 else at < far
+
+                    @pl.when(beyond & has_before[way])
+                    def _():
+                        m_copy(way, at, m_out.at[at]).wait_recv()
+                        m_in[way, at] = m_in[way, at] + m_out[at]
+                        m_copy(way, at, m_in.at[way, at]).start()
+
+                    @pl.when(beyond & jnp.logical_not(has_before[way]))
+                    def _():
+                        m_copy(way, at, m_out.at[at]).start()
+
+                each_far_from_one(one)
+
+    def each_far_from_one(body):
+        lax.fori_loop(1, far_count + 1, lambda j, c: (body(j), c)[1], 0)
+
+    stage(0)
+
+    def later(step):
+        pass_and_add(step)
+        stage(step - 2)
+
+    each_far(3, later)
     if far_count > 2:
-        gram_step(2)
-
-    def later(step):
-        pass_on(step)
-        gram_step(step)
-
-    each_far(3, later)
-
-    m_in[0] = m_out[far]
-    each_far(1, lambda k: m_copy(k).wait_recv())
-    bal_ref[...] = jnp.sum(m_in[:, 0], axis=0)
-    adj_ref[...] = jnp.sum(m_in[:, 1], axis=0)
+        stage(far_count - 2)
+
+    m_out_own = m_out[far]
+    for way in range(2):
+        @pl.when(has_before[way])
+        def _():
+            m_copy(way, far, m_out.at[far]).wait_recv()
+
+        @pl.when(jnp.logical_not(has_before[way]))
+        def _():
+            m_in[way, far] = jnp.zeros_like(m_in[way, far])
+
+        m_out_own = m_out_own + m_in[way, far]
+    bal_ref[...] = m_out_own[0]
+    adj_ref[...] = m_out_own[1]
 
     def g_wait(k):
         source, beside = k // near_count, k % near_count
@@ -242,7 +302,14 @@
         d_copy(k).wait_send()
         r_copy(k).wait_send()
         p_copy(k).wait_send()
-    each_far(1, lambda k: m_copy(k).wait_send())
+
+    def m_left(at):
+        for way in range(2):
+            @pl.when(at > far if way == 0 else at < far)
+            def _():
+                m_copy(way, at, m_out.at[at]).wait_send()
+
+    each_far(0, m_left)
 
     def g_left(k):
         block, beside = k // near_count, k % near_count
@@ -263,15 +330,6 @@
                     a_copy(way, step, chunk, a_ref, far).wait_send()
 
     each_far(0, a_left)
-
-
-def deliver(gram_ref, bal_ref, adj_ref, gram_out, bal_out, adj_out, sem):
-    pairs = ((gram_ref, gram_out), (bal_ref, bal_out), (adj_ref, adj_out))
-    copies = [pltpu.make_async_copy(src, dst, sem.at[i]) for i, (src, dst) in enumerate(pairs)]
-    for copy in copies:
-        copy.start()
-    for copy in copies:
-        copy.wait()
 
 
 def local(direct, adjoint, cell_weight, right_vecs, left_vecs, inv_root):
@@ -285,7 +343,7 @@
     vmem = pl.BlockSpec(memory_space=pltpu.VMEM)
     dma = pltpu.SemaphoreType.DMA
     hbm = pl.BlockSpec(memory_space=pltpu.HBM)
-    results = pl.pallas_call(
+    gram, bal, adj = pl.pallas_call(
         functools.partial(kernel, far_count, near_count, chunks),
         out_shape=(
             jax.ShapeDtypeStruct((near_count, width, width), F32),
@@ -311,7 +369,8 @@
             pltpu.VMEM((near_count, far_count, rows, modes), F32),
             pltpu.VMEM((near_count, far_count, rows, modes), F32),
             pltpu.VMEM((far_count, 2, rows, modes), F32),
-            pltpu.VMEM((far_count, 2, rows, modes), F32),
+            pltpu.VMEM((2, far_count, 2, rows, modes), F32),
+            pltpu.VMEM((2, width, near_count * width), F32),
             dma((2, far_count, chunks)),
             dma((2, far_count, chunks)),
             dma((near_count,)),
@@ -322,8 +381,8 @@
             dma((far_count, near_count)),
             dma((near_count,)),
             dma((near_count,)),
-            dma((far_count,)),
-            dma((far_count,)),
+            dma((2, far_count)),
+            dma((2, far_count)),
         ],
         compiler_params=pltpu.CompilerParams(
             collective_id=0, has_side_effects=True, vmem_limit_bytes=63 * 1024 * 1024
@@ -336,14 +395,6 @@
         left_vecs,
         inv_root.reshape(1, modes),
     )
-    gram, bal, adj = pl.pallas_call(
-        deliver,
-        out_shape=tuple(jax.ShapeDtypeStruct(r.shape, F32) for r in results),
-        in_specs=[hbm] * 3,
-        out_specs=(hbm,) * 3,
-        scratch_shapes=[dma((3,))],
-        compiler_params=pltpu.CompilerParams(vmem_limit_bytes=63 * 1024 * 1024),
-    )(*results)
     return gram.reshape(near_count * width, width), bal, adj
 
 

time: 45.4 us -> 42.6 us (0.938)
  the two profiles are of different devices: /device:TPU:10 before, /device:TPU:0 now
where the time goes in v3:
time: 42.6 us; the launch traced here: 42.4 us
  Pallas kernels  38.7 us (91%)
  local copies, waits for them, and re-layouts  3.09 us (7%)
  between operations  0.65 us (2%)
    pallas_call x1, Pallas kernels, local(): pl.pallas_call(functools.partial(kernel, far_count, near_count, chunks),...  38.7 us
    unnamed x7, local copies, waits for them, and re-layouts  3.09 us

profile of v3, /device:TPU:0, one launch (start us, length us, event | category | flops | bytes accessed | tf_op | source)
XLA Modules:
  0.0 42.4 jit_solution(6680273479507871055)
XLA Ops:
  0.6 38.7 %shard_map.85 = (f32[2,128,128]{2,1,0:T(8,128)}, f32[64,256]{1,0:T(8,128)}, f32[64,256]{1,0:T(8,128)}) custom-call(f32[4,2,64,128]{3,2,1,0:T(8,128)} %bitcast.5, f32[4,2,64,128]{3,2,1,0:T(8,128)} %bitcast.6, f32[1,512]{1,0:T(1,128)} %bitcast.8, f32[128,256]{1,0:T(8,128)} %r_hbm.1, f32[128,256]{1,0:T(8,128)} %l_hbm.1, f32[1,256]{1,0:T(1,128)} %bitcast.9), custom_call_target="tpu_custom_call" | custom-call | tf_op jit(solution)/shard_map/pallas_call | solution.py:346
  39.3 0.0 copy-start.1
  39.3 1.6 %copy.12 = f32[256,128]{1,0:T(8,128)} copy(f32[256,128]{1,0:T(8,128)} %bitcast.7) | data formatting | bytes 262144
  40.9 0.0 copy-done.1
  40.9 0.0 copy-start
  40.9 0.6 %copy.13 = f32[64,256]{1,0:T(8,128)} copy(f32[64,256]{1,0:T(8,128)S(1)} %copy-done.1) | data formatting | bytes 131072
  41.5 0.2 copy-done
  41.8 0.6 %copy.14 = f32[64,256]{1,0:T(8,128)} copy(f32[64,256]{1,0:T(8,128)S(1)} %copy-done) | data formatting | bytes 131072
Async XLA Ops:
  39.3 1.6 %copy-start.1 = (f32[64,256]{1,0:T(8,128)S(1)}, f32[64,256]{1,0:T(8,128)}, u32[]{:S(2)}) copy-start(f32[64,256]{1,0:T(8,128)} %get-tuple-element.13) | copy-start | bytes 196612
  40.9 0.9 %copy-start = (f32[64,256]{1,0:T(8,128)S(1)}, f32[64,256]{1,0:T(8,128)}, u32[]{:S(2)}) copy-start(f32[64,256]{1,0:T(8,128)} %get-tuple-element.14) | copy-start | bytes 196612

commit v4 on v2

--- a/solution.py
+++ b/solution.py
@@ -265,15 +265,6 @@
     each_far(0, a_left)
 
 
-def deliver(gram_ref, bal_ref, adj_ref, gram_out, bal_out, adj_out, sem):
-    pairs = ((gram_ref, gram_out), (bal_ref, bal_out), (adj_ref, adj_out))
-    copies = [pltpu.make_async_copy(src, dst, sem.at[i]) for i, (src, dst) in enumerate(pairs)]
-    for copy in copies:
-        copy.start()
-    for copy in copies:
-        copy.wait()
-
-
 def local(direct, adjoint, cell_weight, right_vecs, left_vecs, inv_root):
     far_count = lax.axis_size("state")
     near_count = lax.axis_size("snap") // far_count
@@ -285,7 +276,7 @@
     vmem = pl.BlockSpec(memory_space=pltpu.VMEM)
     dma = pltpu.SemaphoreType.DMA
     hbm = pl.BlockSpec(memory_space=pltpu.HBM)
-    results = pl.pallas_call(
+    gram, bal, adj = pl.pallas_call(
         functools.partial(kernel, far_count, near_count, chunks),
         out_shape=(
             jax.ShapeDtypeStruct((near_count, width, width), F32),
@@ -336,14 +327,6 @@
         left_vecs,
         inv_root.reshape(1, modes),
     )
-    gram, bal, adj = pl.pallas_call(
-        deliver,
-        out_shape=tuple(jax.ShapeDtypeStruct(r.shape, F32) for r in results),
-        in_specs=[hbm] * 3,
-        out_specs=(hbm,) * 3,
-        scratch_shapes=[dma((3,))],
-        compiler_params=pltpu.CompilerParams(vmem_limit_bytes=63 * 1024 * 1024),
-    )(*results)
     return gram.reshape(near_count * width, width), bal, adj
 
 

time: 45.4 us -> 39.5 us (0.87)
  Pallas kernels: 44.6 us -> 35.5 us
  local copies, waits for them, and re-layouts: 0 us -> 3.09 us
    pallas_call x1 -> x0, Pallas kernels: 9.07 us -> none  [local(): pl.pallas_call(deliver, out_shape=tuple((jax.ShapeDtypeStruct(r.shape, F3...]
    unnamed x0 -> x7, local copies, waits for them, and re-layouts: none -> 3.09 us
where the time goes in v4:
time: 39.5 us; the launch traced here: 39.3 us
  Pallas kernels  35.5 us (90%)
  local copies, waits for them, and re-layouts  3.09 us (8%)
  between operations  0.65 us (2%)
    pallas_call x1, Pallas kernels, local(): pl.pallas_call(functools.partial(kernel, far_count, near_count, chunks),...  35.5 us
    unnamed x7, local copies, waits for them, and re-layouts  3.09 us

profile of v4, /device:TPU:10, one launch (start us, length us, event | category | flops | bytes accessed | tf_op | source)
XLA Modules:
  0.0 39.3 jit_solution(7928810693980390038)
XLA Ops:
  0.6 35.5 %shard_map.85 = (f32[2,128,128]{2,1,0:T(8,128)}, f32[64,256]{1,0:T(8,128)}, f32[64,256]{1,0:T(8,128)}) custom-call(f32[4,2,64,128]{3,2,1,0:T(8,128)} %bitcast.5, f32[4,2,64,128]{3,2,1,0:T(8,128)} %bitcast.6, f32[1,512]{1,0:T(1,128)} %bitcast.8, f32[128,256]{1,0:T(8,128)} %r_hbm.1, f32[128,256]{1,0:T(8,128)} %l_hbm.1, f32[1,256]{1,0:T(1,128)} %bitcast.9), custom_call_target="tpu_custom_call" | custom-call | tf_op jit(solution)/shard_map/pallas_call | solution.py:279
  36.2 0.0 copy-start.1
  36.2 1.6 %copy.12 = f32[256,128]{1,0:T(8,128)} copy(f32[256,128]{1,0:T(8,128)} %bitcast.7) | data formatting | bytes 262144
  37.8 0.0 copy-done.1
  37.8 0.0 copy-start
  37.8 0.6 %copy.13 = f32[64,256]{1,0:T(8,128)} copy(f32[64,256]{1,0:T(8,128)S(1)} %copy-done.1) | data formatting | bytes 131072
  38.4 0.2 copy-done
  38.6 0.6 %copy.14 = f32[64,256]{1,0:T(8,128)} copy(f32[64,256]{1,0:T(8,128)S(1)} %copy-done) | data formatting | bytes 131072
Async XLA Ops:
  36.2 1.6 %copy-start.1 = (f32[64,256]{1,0:T(8,128)S(1)}, f32[64,256]{1,0:T(8,128)}, u32[]{:S(2)}) copy-start(f32[64,256]{1,0:T(8,128)} %get-tuple-element.13) | copy-start | bytes 196612
  37.8 0.9 %copy-start = (f32[64,256]{1,0:T(8,128)S(1)}, f32[64,256]{1,0:T(8,128)}, u32[]{:S(2)}) copy-start(f32[64,256]{1,0:T(8,128)} %get-tuple-element.14) | copy-start | bytes 196612

commit v5 on v4

--- a/solution.py
+++ b/solution.py
@@ -208,8 +208,6 @@
 
         lax.fori_loop(first, far_count, step, 0)
 
-    each_far(1, lambda k: m_copy(k).start())
-
     if far_count > 2:
         gram_step(2)
 
@@ -217,7 +215,23 @@
         pass_on(step)
         gram_step(step)
 
-    each_far(3, later)
+    lax.fori_loop(3, far_count - 1, lambda k, c: (later(k), c)[1], 0)
+    if far_count > 3:
+        pass_on(far_count - 1)
+
+    def a_left(step):
+        for chunk in range(chunks):
+            for way in range(2):
+                block = far - step if way == 0 else far + step
+
+                @pl.when((block >= 0) & (block < far_count) & has_next[way])
+                def _():
+                    a_copy(way, step, chunk, a_ref, far).wait_send()
+
+    each_far(0, a_left)
+    each_far(1, lambda k: m_copy(k).start())
+    if far_count > 3:
+        gram_step(far_count - 1)
 
     m_in[0] = m_out[far]
     each_far(1, lambda k: m_copy(k).wait_recv())
@@ -252,17 +266,6 @@
             g_copy(block, beside).wait_send()
 
     lax.fori_loop(0, far_count * near_count, lambda k, c: (g_left(k), c)[1], 0)
-
-    def a_left(step):
-        for chunk in range(chunks):
-            for way in range(2):
-                block = far - step if way == 0 else far + step
-
-                @pl.when((block >= 0) & (block < far_count) & has_next[way])
-                def _():
-                    a_copy(way, step, chunk, a_ref, far).wait_send()
-
-    each_far(0, a_left)
 
 
 def local(direct, adjoint, cell_weight, right_vecs, left_vecs, inv_root):

time: 39.5 us -> 40.4 us (1.023); the launches traced: 39.3 us -> 39.7 us
  no operation moved by 1% of the time
where the time goes in v5:
time: 40.4 us; the launch traced here: 39.7 us
  Pallas kernels  35.9 us (89%)
  local copies, waits for them, and re-layouts  3.09 us (8%)
  between operations  0.65 us (2%)
    pallas_call x1, Pallas kernels, local(): pl.pallas_call(functools.partial(kernel, far_count, near_count, chunks),...  35.9 us
    unnamed x7, local copies, waits for them, and re-layouts  3.09 us

profile of v5, /device:TPU:10, one launch (start us, length us, event | category | flops | bytes accessed | tf_op | source)
XLA Modules:
  0.0 39.7 jit_solution(10690977023043594802)
XLA Ops:
  0.6 35.9 %shard_map.85 = (f32[2,128,128]{2,1,0:T(8,128)}, f32[64,256]{1,0:T(8,128)}, f32[64,256]{1,0:T(8,128)}) custom-call(f32[4,2,64,128]{3,2,1,0:T(8,128)} %bitcast.5, f32[4,2,64,128]{3,2,1,0:T(8,128)} %bitcast.6, f32[1,512]{1,0:T(1,128)} %bitcast.8, f32[128,256]{1,0:T(8,128)} %r_hbm.1, f32[128,256]{1,0:T(8,128)} %l_hbm.1, f32[1,256]{1,0:T(1,128)} %bitcast.9), custom_call_target="tpu_custom_call" | custom-call | tf_op jit(solution)/shard_map/pallas_call | solution.py:282
  36.6 0.0 copy-start.1
  36.6 1.6 %copy.12 = f32[256,128]{1,0:T(8,128)} copy(f32[256,128]{1,0:T(8,128)} %bitcast.7) | data formatting | bytes 262144
  38.2 0.0 copy-done.1
  38.2 0.0 copy-start
  38.2 0.6 %copy.13 = f32[64,256]{1,0:T(8,128)} copy(f32[64,256]{1,0:T(8,128)S(1)} %copy-done.1) | data formatting | bytes 131072
  38.8 0.2 copy-done
  39.0 0.6 %copy.14 = f32[64,256]{1,0:T(8,128)} copy(f32[64,256]{1,0:T(8,128)S(1)} %copy-done) | data formatting | bytes 131072
Async XLA Ops:
  36.6 1.6 %copy-start.1 = (f32[64,256]{1,0:T(8,128)S(1)}, f32[64,256]{1,0:T(8,128)}, u32[]{:S(2)}) copy-start(f32[64,256]{1,0:T(8,128)} %get-tuple-element.13) | copy-start | bytes 196612
  38.2 0.9 %copy-start = (f32[64,256]{1,0:T(8,128)S(1)}, f32[64,256]{1,0:T(8,128)}, u32[]{:S(2)}) copy-start(f32[64,256]{1,0:T(8,128)} %get-tuple-element.14) | copy-start | bytes 196612
